TPU v7x, 32 devices: a whole 2x2x4 slice. The times are simulated.
32 devices in a mesh: groups: 2 (over y), tok: 4 (over x, core), hid: 4 (over z).
Axes of the slice: x: 2, y: 2, z: 4, core: 2. Of those that a mesh axis runs over, the one named last changes fastest.
Arguments:
- states: bfloat16 [8192, 5376], P(('groups', 'tok'), 'hid'), parts along dimension 0, may hold values from -6 to 6
- w_qkv: bfloat16 [5376, 8, 512], P('tok', 'hid'), may hold values from -0.078125 to 0.078125
- w_out: bfloat16 [2048, 5376], P('tok', 'hid'), may hold values from -0.125 to 0.125
- q_gain: float32 [128], replicated, may hold values from 0.5 to 14, as said below
- k_gain: float32 [128], replicated, may hold values from 0.5 to 14, as said below
Outputs:
- attended: bfloat16 [8192, 5376], P(('groups', 'tok'), 'hid'), parts along dimension 0
There are 2 independent parts, one for each index of `groups`. A program takes and returns all parts, laid end to end along the dimension named above; an argument that names none is the same for every part. Nothing has to cross between parts.
Inputs may be any that keep to these rules, and one draw needn't show every extreme that they name: `q_gain`: entries are positive. `k_gain`: entries are positive.
All inputs are finite; a program needn't handle non-finite values.
Results may differ from a plain program's by a relative error of at most 0.017.
The roundings to bfloat16 on the way count: a program that leaves them out, or rounds other values in their place, can miss the bound.
Values may be sent and summed in bfloat16 or wider, within the bound.
A program may use at most 128 MiB of HBM per device.

v0:
```python
import math
import jax
import jax.numpy as jnp
from jax import lax
from jax.sharding import PartitionSpec as P

HD = 128
GROUP = 2
WINDOW = 1024
EPS = 1e-06
SCALE = 168.0 ** (-0.5)
ROPE_BASE = 10000.0


def from_behind(value, axis, steps):
    count = lax.axis_size(axis)
    first, last = (max(0, -steps), min(count, count - steps))
    return lax.ppermute(value, axis, [(source, source + steps) for source in range(first, last)])


def head_norm(values, gain):
    meansq = jnp.mean(values * values, axis=-1, keepdims=True)
    return values * lax.rsqrt(meansq + EPS) * gain


def rotate(values, pos):
    half = values.shape[-1] // 2
    inverse = jnp.exp(
        jnp.arange(half, dtype=jnp.float32) * (-2.0 * math.log(ROPE_BASE) / values.shape[-1])
    )
    angle = pos.astype(jnp.float32)[:, None] * inverse[None, :]
    shape = (angle.shape[0],) + (1,) * (values.ndim - 2) + (half,)
    cosine = jnp.cos(angle).reshape(shape)
    sine = jnp.sin(angle).reshape(shape)
    first = values[..., :half]
    second = values[..., half:]
    return jnp.concatenate(
        [first * cosine - second * sine, second * cosine + first * sine], axis=-1
    )


def attend(query, keys, values, q_first, k_first):
    scores = jnp.einsum("qhgd,khd->hgqk", query, keys, preferred_element_type=jnp.float32) * SCALE
    q_index = q_first + jnp.arange(query.shape[0], dtype=jnp.int32)
    k_index = k_first + jnp.arange(keys.shape[0], dtype=jnp.int32)
    keep = (
        (k_index[None, :] <= q_index[:, None])
        & (q_index[:, None] - k_index[None, :] < WINDOW)
        & (k_index[None, :] >= 0)
    )
    masked = jnp.where(keep, scores, jnp.float32(-1e30))
    top = jnp.max(masked, axis=-1, keepdims=True)
    expo = jnp.where(keep, jnp.exp(masked - top), jnp.float32(0.0))
    total = jnp.sum(expo, axis=-1, keepdims=True)
    weights = (expo / total).astype(jnp.bfloat16)
    result = jnp.einsum("hgqk,khd->qhgd", weights, values, preferred_element_type=jnp.float32)
    return result.astype(jnp.bfloat16)


def on_device(states, w_qkv, w_out, q_gain, k_gain):
    rows = states.shape[0]
    kv_local = w_qkv.shape[1]
    columns = kv_local * (GROUP + 2) * HD
    weight_whole = lax.all_gather(w_qkv, "tok", axis=0, tiled=True).reshape(-1, columns)
    weight_part = weight_whole
    qkv = jnp.dot(
        lax.all_gather(states, "hid", axis=1, tiled=True),
        weight_part,
        preferred_element_type=jnp.float32,
    )
    qkv = qkv.reshape(rows, kv_local, GROUP + 2, HD)
    base = lax.axis_index("tok") * rows
    pos = base + jnp.arange(rows, dtype=jnp.int32)
    query = rotate(head_norm(qkv[:, :, :GROUP], q_gain), pos).astype(jnp.bfloat16)
    keys = rotate(head_norm(qkv[:, :, GROUP], k_gain), pos).astype(jnp.bfloat16)
    values = qkv[:, :, GROUP + 1].astype(jnp.bfloat16)
    paired = jnp.stack([keys, values], axis=1).reshape(rows, 2 * kv_local * HD)
    hops = max(1, WINDOW // rows)
    reach = min(WINDOW, rows)
    pieces = []
    current = paired
    current = from_behind(current, "tok", 1)
    pieces.insert(0, current)
    combined = jnp.concatenate(pieces + [paired], axis=0).reshape(-1, 2, kv_local, HD)
    reach_back = hops * reach
    block = 512
    outputs = []
    for index in range(rows // block):
        q_block = query[index * block : (index + 1) * block]
        kv_block = combined[index * block : index * block + block + reach_back]
        outputs.append(
            attend(
                q_block,
                kv_block[:, 0],
                kv_block[:, 1],
                base + index * block,
                base + index * block - reach_back,
            )
        )
    heads_out = jnp.concatenate(outputs, axis=0)
    heads_out = heads_out.reshape(rows, kv_local * GROUP * HD)
    out_whole = lax.all_gather(w_out, "tok", axis=0, tiled=True)
    weight_part = out_whole
    summed = jnp.dot(
        lax.all_gather(heads_out, "hid", axis=1, tiled=True),
        weight_part,
        preferred_element_type=jnp.float32,
    )
    return summed.astype(jnp.bfloat16)


def solution(mesh):
    return jax.shard_map(
        on_device,
        mesh=mesh,
        in_specs=(P(("groups", "tok"), "hid"), P("tok", "hid", None), P("tok", "hid"), P(), P()),
        out_specs=P(("groups", "tok"), "hid"),
        check_vma=False,
    )
```

profile of v0, /device:TPU:0, one launch (start us, length us, event | category | flops | bytes accessed | tf_op | source)
XLA Modules:
  0.0 458.9 jit_solution(5258725831197770475)
XLA Ops:
  6.5 0.0 all-gather.7.cloned.1.call-start
  6.5 0.7 all-gather.7.cloned.1.call-update
  7.3 0.0 all-gather.5.cloned.1.call-start
  7.3 0.7 all-gather.5.cloned.1.call-update
  8.0 0.0 all-gather.11.cloned.1.call-start
  8.1 0.7 all-gather.11.cloned.1.call-update
  8.7 0.0 all-gather.9.cloned.1.call-start
  8.9 1.0 multiply_cosine_fusion
  9.9 1.9 fusion.15
  11.8 1.9 fusion.17
  13.7 71.1 %all-gather.7.cloned.1.call-done = bf16[5376,2,512]{2,1,0:T(2,128)(2,1)} async-done(((bf16[1344,2,512]{2,1,0:T(2,128)(2,1)}), bf16[5376,2,512]{2,1,0:T(2,128)(2,1)}) %all-gather.7.cloned.1.call-update) | async-done | bytes 11010064 | tf_op jit(solution)/shard_map/all_gather | solution.py:64
  84.8 27.7 %copy.39 = bf16[5376,2,512]{0,2,1:T(8,128)(2,1)} copy(bf16[5376,2,512]{2,1,0:T(2,128)(2,1)} %all-gather.7.cloned.1.call-done) | data formatting | bytes 22020096 | tf_op jit(solution)/shard_map/reshape | solution.py:64
  112.5 166.4 %all-gather.5.cloned.1.call-done = bf16[1024,5376]{0,1:T(8,128)(2,1)} async-done(((bf16[1024,1344]{0,1:T(8,128)(2,1)}), bf16[1024,5376]{0,1:T(8,128)(2,1)}) %all-gather.5.cloned.1.call-update) | async-done | bytes 11010064 | tf_op jit(solution)/shard_map/all_gather | solution.py:67
  278.9 0.0 copy-start
  278.9 15.9 %fusion.2 = f32[1024,2,4,128]{0,3,2,1:T(8,128)S(1)} fusion(bf16[2,4,128,5376]{3,2,1,0:T(8,128)(2,1)} %bitcast.101, bf16[1024,5376]{0,1:T(8,128)(2,1)} %all-gather.5.cloned.1.call-done), kind=kOutput, calls=%fused_computation.8 | convolution fusion | flops 11274289152 | bytes 26214400 | tf_op jit(solution)/shard_map/dot_general | solution.py:66
  294.9 0.1 multiply_reduce_fusion.1
  295.0 0.1 fusion.30
  295.1 0.0 copy-done
  295.1 0.0 copy-start.1
  295.1 0.2 multiply_multiply_fusion.1
  295.3 0.2 fusion.31
  295.5 0.1 pad_maximum_fusion.1
  295.5 2.2 collective-permute-start
  297.8 0.2 multiply_reduce_fusion
  298.0 0.0 copy-done.1
  298.0 0.4 multiply_multiply_fusion
  298.5 1.4 subtract_convert_fusion
  299.9 0.1 collective-permute-done
  300.0 0.2 fusion.18
  300.2 10.3 %fusion.45 = (f32[2,2,512]{2,1,0:T(2,128)S(1)}, f32[2,2,512,1536]{2,3,1,0:T(8,128)}) fusion(pred[512,1536]{0,1:T(8,128)(4,1)} %fusion.17, bf16[1536,2,2,128]{0,3,2,1:T(8,128)(2,1)S(1)} %bitcast.105, bf16[1024,2,2,64]{0,3,2,1:T(8,128)(2,1)} %get-tuple-element.6, bf16[1024,2,2,64]{0,3,2,1:T(8,128)(2,1)} %get-tuple-element.5), kind=kOutput, calls=%fused_computation.80 | convolution fusion | flops 822085120 | bytes 15998976 | tf_op jit(solution)/shard_map/sub | solution.py:53
  310.6 10.2 %fusion.46 = (f32[2,2,512]{2,1,0:T(2,128)S(1)}, f32[2,2,512,1536]{2,3,1,0:T(8,128)}) fusion(pred[512,1536]{0,1:T(8,128)(4,1)} %fusion.15, bf16[1536,2,2,128]{0,3,2,1:T(8,128)(2,1)S(1)} %bitcast.107, bf16[1024,2,2,64]{0,3,2,1:T(8,128)(2,1)} %get-tuple-element.5, bf16[1024,2,2,64]{0,3,2,1:T(8,128)(2,1)} %get-tuple-element.6), kind=kOutput, calls=%fused_computation.81 | convolution fusion | flops 822085120 | bytes 15998976 | tf_op jit(solution)/shard_map/sub | solution.py:53
  320.8 0.0 copy-start.2
  320.8 5.7 %fusion.25 = bf16[512,2,2,128]{0,3,2,1:T(8,128)(2,1)S(1)} fusion(f32[2,2,512,1536]{2,3,1,0:T(8,128)} %get-tuple-element.16, f32[2,2,512]{2,1,0:T(2,128)S(1)} %get-tuple-element.15, bf16[1536,2,2,128]{0,3,2,1:T(8,128)(2,1)S(1)} %bitcast.108), kind=kOutput, calls=%fused_computation.37 | convolution fusion | flops 811859968 | bytes 13901824 | tf_op jit(solution)/shard_map/hgqk,khd->qhgd/dot_general | solution.py:56
  326.5 2.4 copy-done.2
  329.0 1.0 fusion.26
  330.0 1.1 pad_maximum_fusion.2
  331.1 0.0 all-gather.9.cloned.1.call-update
  331.1 0.0 all-gather.11.cloned.1.call-done
  331.1 111.1 %all-gather.9.cloned.1.call-done = bf16[1024,2048]{0,1:T(8,128)(2,1)} async-done(((bf16[1024,512]{0,1:T(8,128)(2,1)}), bf16[1024,2048]{0,1:T(8,128)(2,1)}) %all-gather.9.cloned.1.call-update) | async-done | bytes 4194320 | tf_op jit(solution)/shard_map/all_gather | solution.py:105
  442.3 10.1 %convolution_convert_fusion = bf16[1024,1344]{0,1:T(8,128)(2,1)} fusion(bf16[2048,1344]{0,1:T(8,128)(2,1)} %all-gather.11.cloned.1.call-done, bf16[1024,2048]{0,1:T(8,128)(2,1)} %all-gather.9.cloned.1.call-done), kind=kOutput, calls=%fused_computation.20 | convolution fusion | flops 5638520832 | bytes 12451840 | tf_op jit(solution)/shard_map/dot_general | solution.py:104
  (10 shorter events, 0.1 us)
Async XLA Ops:
  6.5 78.3 %all-gather.7.cloned.1.call-start = ((), (), s32[]{:S(2)}) async-start(), calls=%async_computation.1 | async-start | bytes 13762560 | tf_op jit(solution)/shard_map/all_gather | solution.py:64
  7.3 271.7 %all-gather.5.cloned.1.call-start = ((), (), s32[]{:S(2)}) async-start(), calls=%async_computation | async-start | bytes 13762560 | tf_op jit(solution)/shard_map/all_gather | solution.py:67
  8.0 323.1 %all-gather.11.cloned.1.call-start = ((), (), s32[]{:S(2)}) async-start(), calls=%async_computation.3 | async-start | bytes 6881280 | tf_op jit(solution)/shard_map/all_gather | solution.py:102
  8.7 433.5 %all-gather.9.cloned.1.call-start = ((), (), s32[]{:S(2)}) async-start(), calls=%async_computation.2 | async-start | bytes 5242880 | tf_op jit(solution)/shard_map/all_gather | solution.py:105
  278.9 16.2 %copy-start = (f32[128]{0:T(128)S(1)}, f32[128]{0:T(128)}, u32[]{:S(2)}) copy-start(f32[128]{0:T(128)} %param.9) | copy-start | bytes 1540
  295.1 3.0 copy-start.1
  295.5 4.4 collective-permute-start
  320.8 8.2 %copy-start.2 = (f32[2,2,512,1536]{2,3,1,0:T(8,128)S(1)}, f32[2,2,512,1536]{2,3,1,0:T(8,128)}, u32[]{:S(2)}) copy-start(f32[2,2,512,1536]{2,3,1,0:T(8,128)} %get-tuple-element.14) | copy-start | bytes 37748740
Sparse Core Ops, SparseCore 0:
  8.9 75.8 all-gather.6
  86.4 192.4 all-gather.4
  280.5 45.1 all-gather.10
  331.2 110.9 all-gather.8
where the time goes:
time: 460 us; the launch traced here: 459 us
  waiting for transfers between devices  351 us (76%)
  matrix products  53.4 us (12%)
  local copies, waits for them, and re-layouts  30.2 us (7%)
  between operations  13.3 us (3%)
  other arithmetic  8.83 us (2%)
    all_gather x1, waiting for transfers between devices, on_device(): lax.all_gather(states, 'hid', axis=1, tiled=True)  166 us
    all_gather x1, waiting for transfers between devices, on_device(): lax.all_gather(heads_out, 'hid', axis=1, tiled=True)  111 us
    all_gather x1, waiting for transfers between devices, on_device(): lax.all_gather(w_qkv, 'tok', axis=0, tiled=True).reshape(-1, columns)  71.1 us
    reshape x1, local copies, waits for them, and re-layouts, on_device(): lax.all_gather(w_qkv, 'tok', axis=0, tiled=True).reshape(-1, columns)  27.7 us
    sub x2, matrix products, attend(): expo = jnp.where(keep, jnp.exp(masked - top), jnp.float32(0.0))  20.6 us
    dot_general x1, matrix products, on_device(): jnp.dot(lax.all_gather(states, 'hid', axis=1, tiled=True), weight_part, p...  15.9 us
    dot_general x1, matrix products, on_device(): jnp.dot(lax.all_gather(heads_out, 'hid', axis=1, tiled=True), weight_part...  10.1 us
  transfers between devices with their start and end apart: 5, of which 4 were waited for; matrix products, arithmetic and copies ran while one was open for 17% of the time, Pallas kernels for 0%

commit v1 on v0

--- a/solution.py
+++ b/solution.py
@@ -10,6 +10,19 @@
 EPS = 1e-06
 SCALE = 168.0 ** (-0.5)
 ROPE_BASE = 10000.0
+
+
+def collect(x, axis, dim):
+    ways = lax.axis_size(axis)
+    up = [(d, (d + 1) % ways) for d in range(ways)]
+    down = [(d, (d - 1) % ways) for d in range(ways)]
+    earlier, later = ([x], [x])
+    for _ in range(ways // 2):
+        earlier.append(lax.ppermute(earlier[-1], axis, up))
+    for _ in range((ways - 1) // 2):
+        later.append(lax.ppermute(later[-1], axis, down))
+    line = jnp.concatenate([*earlier[::-1], *later[1:]], axis=dim)
+    return jnp.roll(line, (lax.axis_index(axis) - ways // 2) * x.shape[dim], axis=dim)
 
 
 def from_behind(value, axis, steps):
@@ -63,11 +76,7 @@
     columns = kv_local * (GROUP + 2) * HD
     weight_whole = lax.all_gather(w_qkv, "tok", axis=0, tiled=True).reshape(-1, columns)
     weight_part = weight_whole
-    qkv = jnp.dot(
-        lax.all_gather(states, "hid", axis=1, tiled=True),
-        weight_part,
-        preferred_element_type=jnp.float32,
-    )
+    qkv = jnp.dot(collect(states, "hid", 1), weight_part, preferred_element_type=jnp.float32)
     qkv = qkv.reshape(rows, kv_local, GROUP + 2, HD)
     base = lax.axis_index("tok") * rows
     pos = base + jnp.arange(rows, dtype=jnp.int32)

time: 460 us -> 430 us (0.935)
  waiting for transfers between devices: 351 us -> 254 us
  local copies, waits for them, and re-layouts: 30.2 us -> 88.5 us
    all_gather x1 -> x0, waiting for transfers between devices: 166 us -> none  [on_device(): lax.all_gather(states, 'hid', axis=1, tiled=True)]
    ppermute x0 -> x3, waiting for transfers between devices: none -> 161 us  [the longest x2 116 us: collect(): earlier.append(lax.ppermute(earlier[-1], axis, up))]
    all_gather x1, waiting for transfers between devices: 71.1 us -> 0.01 us  [on_device(): lax.all_gather(w_qkv, 'tok', axis=0, tiled=True).reshape(-1, columns)]
    concatenate x0 -> x1, local copies, waits for them, and re-layouts: none -> 41.7 us  [collect(): jnp.roll(line, (lax.axis_index(axis) - ways // 2) * x.shape[dim], axis=dim)]
    all_gather x1, waiting for transfers between devices: 111 us -> 92.6 us  [on_device(): lax.all_gather(heads_out, 'hid', axis=1, tiled=True)]
    ppermute x0 -> x3, local copies, waits for them, and re-layouts: none -> 13.6 us  [the longest x2 9.06 us: collect(): earlier.append(lax.ppermute(earlier[-1], axis, up))]
    ppermute x0 -> x3, starting transfers between devices: none -> 5.17 us  [the longest x2 3.08 us: collect(): earlier.append(lax.ppermute(earlier[-1], axis, up))]
  transfers between devices with their start and end apart: 5 -> 7, of which waited for: 4 -> 4; matrix products, arithmetic and copies ran while one was open for 17% -> 33% of each run, Pallas kernels for 0% -> 0%
where the time goes in v1:
time: 430 us; the launch traced here: 425 us
  waiting for transfers between devices  254 us (59%)
  local copies, waits for them, and re-layouts  88.5 us (21%)
  matrix products  53.3 us (12%)
  between operations  13.4 us (3%)
  other arithmetic  8.84 us (2%)
  starting transfers between devices  6.79 us (2%)
    ppermute x2, waiting for transfers between devices, collect(): earlier.append(lax.ppermute(earlier[-1], axis, up))  116 us
    all_gather x1, waiting for transfers between devices, on_device(): lax.all_gather(heads_out, 'hid', axis=1, tiled=True)  92.6 us
    ppermute x1, waiting for transfers between devices, collect(): later.append(lax.ppermute(later[-1], axis, down))  44.9 us
    concatenate x1, local copies, waits for them, and re-layouts, collect(): jnp.roll(line, (lax.axis_index(axis) - ways // 2) * x.shape[dim], axis=dim)  41.7 us
    reshape x1, local copies, waits for them, and re-layouts, on_device(): lax.all_gather(w_qkv, 'tok', axis=0, tiled=True).reshape(-1, columns)  27.4 us
    sub x2, matrix products, attend(): expo = jnp.where(keep, jnp.exp(masked - top), jnp.float32(0.0))  20.6 us
    dot_general x1, matrix products, on_device(): jnp.dot(collect(states, 'hid', 1), weight_part, preferred_element_type=jn...  15.9 us
    dot_general x1, matrix products, on_device(): jnp.dot(lax.all_gather(heads_out, 'hid', axis=1, tiled=True), weight_part...  10.1 us
  transfers between devices with their start and end apart: 7, of which 4 were waited for; matrix products, arithmetic and copies ran while one was open for 33% of the time, Pallas kernels for 0%

profile of v1, /device:TPU:0, one launch (start us, length us, event | category | flops | bytes accessed | tf_op | source)
XLA Modules:
  0.0 424.8 jit_solution(5283161865980007829)
XLA Ops:
  6.5 0.0 all-gather.4.cloned.1.call-start
  6.5 0.7 all-gather.4.cloned.1.call-update
  7.3 0.0 all-gather.8.cloned.1.call-start
  7.3 3.1 collective-permute-start
  10.4 2.1 collective-permute-start.2
  12.5 60.8 %collective-permute-done = bf16[1024,1344]{0,1:T(8,128)(2,1)} collective-permute-done((bf16[1024,1344]{0,1:T(8,128)(2,1)}, bf16[1024,1344]{0,1:T(8,128)(2,1)}, u32[]{:S(2)}, u32[]{:S(2)}) %collective-permute-start) | collective-permute-done | bytes 2752544 | tf_op jit(solution)/shard_map/ppermute | solution.py:21
  73.3 0.0 collective-permute-start.1
  73.3 0.0 all-gather.8.cloned.1.call-update
  73.3 0.0 all-gather.6.cloned.1.call-start
  73.4 3.3 copy.32
  76.8 1.0 multiply_cosine_fusion
  77.8 1.9 fusion.16
  79.7 1.9 fusion.18
  81.6 4.5 %copy.31 = bf16[1024,1344]{1,0:T(8,128)(2,1)} copy(bf16[1024,1344]{0,1:T(8,128)(2,1)} %collective-permute-done) | data formatting | bytes 5505024 | tf_op jit(solution)/shard_map/ppermute | solution.py:21
  86.1 44.9 %collective-permute-done.2 = bf16[1024,1344]{0,1:T(8,128)(2,1)} collective-permute-done((bf16[1024,1344]{0,1:T(8,128)(2,1)}, bf16[1024,1344]{0,1:T(8,128)(2,1)}, u32[]{:S(2)}, u32[]{:S(2)}) %collective-permute-start.2) | collective-permute-done | bytes 2752544 | tf_op jit(solution)/shard_map/ppermute | solution.py:23
  131.0 4.5 %copy.33 = bf16[1024,1344]{1,0:T(8,128)(2,1)} copy(bf16[1024,1344]{0,1:T(8,128)(2,1)} %collective-permute-done.2) | data formatting | bytes 5505024 | tf_op jit(solution)/shard_map/ppermute | solution.py:23
  135.5 54.9 %collective-permute-done.1 = bf16[1024,1344]{0,1:T(8,128)(2,1)} collective-permute-done((bf16[1024,1344]{0,1:T(8,128)(2,1)}, bf16[1024,1344]{0,1:T(8,128)(2,1)}, u32[]{:S(2)}, u32[]{:S(2)}) %collective-permute-start.1) | collective-permute-done | bytes 2752544 | tf_op jit(solution)/shard_map/ppermute | solution.py:21
  190.4 4.5 %copy.30 = bf16[1024,1344]{1,0:T(8,128)(2,1)} copy(bf16[1024,1344]{0,1:T(8,128)(2,1)} %collective-permute-done.1) | data formatting | bytes 5505024 | tf_op jit(solution)/shard_map/ppermute | solution.py:21
  194.9 41.7 %concatenate.31 = bf16[1024,10752]{1,0:T(8,128)(2,1)} concatenate(bf16[1024,1344]{1,0:T(8,128)(2,1)} %copy.30, bf16[1024,1344]{1,0:T(8,128)(2,1)} %copy.31, bf16[1024,1344]{1,0:T(8,128)(2,1)S(1)} %copy.32, bf16[1024,1344]{1,0:T(8,128)(2,1)} %copy.33, bf16[1024,1344]{1,0:T(8,128)(2,1)} %copy.30, bf16[1024,1344]{1,0:T(8,128)(2,1)} %copy.31, bf16[1024,1344]{1,0:T(8,128)(2,1)S(1)} %copy.32, ...), dimensions={1} | concatenate | bytes 44040192 | tf_op jit(solution)/shard_map/jit(_roll_dynamic)/concatenate | solution.py:25
  236.6 0.0 all-gather.4.cloned.1.call-done
  236.7 27.4 %copy.55 = bf16[5376,2,512]{0,2,1:T(8,128)(2,1)} copy(bf16[5376,2,512]{2,1,0:T(2,128)(2,1)} %all-gather.4.cloned.1.call-done) | data formatting | bytes 22020096 | tf_op jit(solution)/shard_map/reshape | solution.py:77
  264.1 0.0 copy-start
  264.1 15.9 %fusion.2 = f32[1024,2,4,128]{0,3,2,1:T(8,128)S(1)} fusion(bf16[2,4,128,5376]{3,2,1,0:T(8,128)(2,1)} %bitcast.101, bf16[1024,10752]{1,0:T(8,128)(2,1)} %concatenate.31, s32[]{:T(128)S(6)} %select_n.27), kind=kOutput, calls=%fused_computation.8 | convolution fusion | flops 11274289152 | bytes 26214404 | tf_op jit(solution)/shard_map/dot_general | solution.py:79
  279.9 0.1 multiply_reduce_fusion.1
  280.1 0.1 fusion.31
  280.2 0.0 copy-done
  280.2 0.2 multiply_multiply_fusion.1
  280.4 0.0 copy-start.1
  280.4 0.2 fusion.32
  280.5 0.1 pad_maximum_fusion.1
  280.6 1.5 collective-permute-start.3
  282.2 0.2 multiply_reduce_fusion
  282.4 0.0 copy-done.1
  282.4 0.4 multiply_multiply_fusion
  282.9 1.4 subtract_convert_fusion
  284.3 0.0 collective-permute-done.3
  284.3 0.2 fusion.19
  284.5 10.3 %fusion.47 = (f32[2,2,512]{2,1,0:T(2,128)S(1)}, f32[2,2,512,1536]{2,3,1,0:T(8,128)}) fusion(pred[512,1536]{0,1:T(8,128)(4,1)} %fusion.18, bf16[1536,2,2,128]{0,3,2,1:T(8,128)(2,1)S(1)} %bitcast.105, bf16[1024,2,2,64]{0,3,2,1:T(8,128)(2,1)} %get-tuple-element.6, bf16[1024,2,2,64]{0,3,2,1:T(8,128)(2,1)} %get-tuple-element.5), kind=kOutput, calls=%fused_computation.82 | convolution fusion | flops 822085120 | bytes 15998976 | tf_op jit(solution)/shard_map/sub | solution.py:66
  294.9 10.2 %fusion.48 = (f32[2,2,512]{2,1,0:T(2,128)S(1)}, f32[2,2,512,1536]{2,3,1,0:T(8,128)}) fusion(pred[512,1536]{0,1:T(8,128)(4,1)} %fusion.16, bf16[1536,2,2,128]{0,3,2,1:T(8,128)(2,1)S(1)} %bitcast.107, bf16[1024,2,2,64]{0,3,2,1:T(8,128)(2,1)} %get-tuple-element.5, bf16[1024,2,2,64]{0,3,2,1:T(8,128)(2,1)} %get-tuple-element.6), kind=kOutput, calls=%fused_computation.83 | convolution fusion | flops 822085120 | bytes 15998976 | tf_op jit(solution)/shard_map/sub | solution.py:66
  305.1 0.0 copy-start.2
  305.1 5.7 %fusion.26 = bf16[512,2,2,128]{0,3,2,1:T(8,128)(2,1)S(1)} fusion(f32[2,2,512,1536]{2,3,1,0:T(8,128)} %get-tuple-element.16, f32[2,2,512]{2,1,0:T(2,128)S(1)} %get-tuple-element.15, bf16[1536,2,2,128]{0,3,2,1:T(8,128)(2,1)S(1)} %bitcast.108), kind=kOutput, calls=%fused_computation.38 | convolution fusion | flops 811859968 | bytes 13901824 | tf_op jit(solution)/shard_map/hgqk,khd->qhgd/dot_general | solution.py:69
  310.9 2.4 copy-done.2
  313.3 1.0 fusion.27
  314.3 1.1 pad_maximum_fusion.2
  315.4 0.0 all-gather.6.cloned.1.call-update
  315.4 0.0 all-gather.8.cloned.1.call-done
  315.5 92.6 %all-gather.6.cloned.1.call-done = bf16[1024,2048]{0,1:T(8,128)(2,1)} async-done(((bf16[1024,512]{0,1:T(8,128)(2,1)}), bf16[1024,2048]{0,1:T(8,128)(2,1)}) %all-gather.6.cloned.1.call-update) | async-done | bytes 4194320 | tf_op jit(solution)/shard_map/all_gather | solution.py:114
  408.1 10.1 %convolution_convert_fusion = bf16[1024,1344]{0,1:T(8,128)(2,1)} fusion(bf16[2048,1344]{0,1:T(8,128)(2,1)} %all-gather.8.cloned.1.call-done, bf16[1024,2048]{0,1:T(8,128)(2,1)} %all-gather.6.cloned.1.call-done), kind=kOutput, calls=%fused_computation.21 | convolution fusion | flops 5638520832 | bytes 12451840 | tf_op jit(solution)/shard_map/dot_general | solution.py:113
  (10 shorter events, 0.1 us)
Async XLA Ops:
  6.5 230.1 %all-gather.4.cloned.1.call-start = ((), (), s32[]{:S(2)}) async-start(), calls=%async_computation | async-start | bytes 13762560 | tf_op jit(solution)/shard_map/all_gather | solution.py:77
  7.3 308.2 %all-gather.8.cloned.1.call-start = ((), (), s32[]{:S(2)}) async-start(), calls=%async_computation.2 | async-start | bytes 6881280 | tf_op jit(solution)/shard_map/all_gather | solution.py:111
  7.3 66.0 %collective-permute-start = (bf16[1024,1344]{0,1:T(8,128)(2,1)}, bf16[1024,1344]{0,1:T(8,128)(2,1)}, u32[]{:S(2)}, u32[]{:S(2)}) collective-permute-start(bf16[1024,1344]{0,1:T(8,128)(2,1)} %param.5), channel_id=1, source_target_pairs={{0,1},{1,2},{2,3},{3,0},{4,5},{5,6},{6,7},{7,4},{8,9},{9,10},{10,1... | collective-permute-start | bytes 8257544 | tf_op jit(solution)/shard_map/ppermute | solution.py:21
  10.4 120.6 %collective-permute-start.2 = (bf16[1024,1344]{0,1:T(8,128)(2,1)}, bf16[1024,1344]{0,1:T(8,128)(2,1)}, u32[]{:S(2)}, u32[]{:S(2)}) collective-permute-start(bf16[1024,1344]{0,1:T(8,128)(2,1)} %param.5), channel_id=1, source_target_pairs={{0,3},{1,0},{2,1},{3,2},{4,7},{5,4},{6,5},{7,6},{8,11},{9,8},{10,9... | collective-permute-start | bytes 8257544 | tf_op jit(solution)/shard_map/ppermute | solution.py:23
  73.3 117.1 %collective-permute-start.1 = (bf16[1024,1344]{0,1:T(8,128)(2,1)}, bf16[1024,1344]{0,1:T(8,128)(2,1)}, u32[]{:S(2)}, u32[]{:S(2)}) collective-permute-start(bf16[1024,1344]{0,1:T(8,128)(2,1)} %collective-permute-done), channel_id=1, source_target_pairs={{0,1},{1,2},{2,3},{3,0},{4,5},{5,6},{6,7},{7,4},{8,9},{9,10},{10,1... | collective-permute-start | bytes 8257544 | tf_op jit(solution)/shard_map/ppermute | solution.py:21
  73.3 334.8 %all-gather.6.cloned.1.call-start = ((), (), s32[]{:S(2)}) async-start(), calls=%async_computation.1 | async-start | bytes 5242880 | tf_op jit(solution)/shard_map/all_gather | solution.py:114
  264.1 16.1 %copy-start = (f32[128]{0:T(128)S(1)}, f32[128]{0:T(128)}, u32[]{:S(2)}) copy-start(f32[128]{0:T(128)} %param.9) | copy-start | bytes 1540
  280.4 2.1 copy-start.1
  280.6 3.7 collective-permute-start.3
  305.1 8.2 %copy-start.2 = (f32[2,2,512,1536]{2,3,1,0:T(8,128)S(1)}, f32[2,2,512,1536]{2,3,1,0:T(8,128)}, u32[]{:S(2)}) copy-start(f32[2,2,512,1536]{2,3,1,0:T(8,128)} %get-tuple-element.14) | copy-start | bytes 37748740
Sparse Core Ops, SparseCore 0:
  8.9 75.8 all-gather.3
  86.4 86.0 all-gather.7
  315.5 92.4 all-gather.5
